TPU v7x, 32 devices: a whole 2x2x4 slice. The times are simulated.
32 devices in a mesh: rep: 4 (over z), fsdp: 8 (over y, x, core).
Axes of the slice: x: 2, y: 2, z: 4, core: 2. Of those that a mesh axis runs over, the one named last changes fastest.
Arguments:
- grads: bfloat16 [4, 8, 768, 2048], P('rep', None, 'fsdp'), may hold values from -400 to 400
- momentum: float32 [8, 8, 96, 2048], P('fsdp', None, 'rep'), may hold values from -384 to 384
- owner: int32 [8], replicated, may hold values from 0 to 7, each once
Outputs:
- update: bfloat16 [8, 8, 96, 2048], P(None, 'fsdp', 'rep')
- momentum_out: float32 [8, 8, 96, 2048], P('fsdp', None, 'rep')
Inputs may be any that keep to these rules, and one draw needn't show every extreme that they name: `owner`: every slot holds exactly one expert.
All inputs are finite; a program needn't handle non-finite values.
Results may differ from a plain program's by a relative error of at most 0.012.
Values may be sent and summed in bfloat16 or wider, within the bound.
A program may use at most 64 MiB of HBM per device.

v0:
```python
import math

import jax
import jax.numpy as jnp
from jax import lax
from jax.sharding import PartitionSpec as P

D = 2048
ITERS = 2


DECAY_RATE = 0.95
NEWTON_A = 3.4445
NEWTON_B = -4.775
NEWTON_C = 2.0315
EPSILON = 1e-07


def finish_rows(own_gram, gram_matrix):
    squared = jnp.dot(own_gram, gram_matrix, preferred_element_type=jnp.float32)
    polynomial = (NEWTON_B * own_gram.astype(jnp.float32) + NEWTON_C * squared).astype(jnp.bfloat16)
    return polynomial


def rows_whole(current, first_row):
    slab_rows = current.shape[0]
    result = current.astype(jnp.float32)
    for iteration in range(ITERS):
        gathered = lax.all_gather(current, "rep", axis=0, tiled=True)
        if iteration == 0:
            values = gathered.astype(jnp.float32)
            frobenius = jnp.sqrt(jnp.sum(values * values))
            whole = (values / (frobenius + EPSILON)).astype(jnp.bfloat16)
            mine = lax.dynamic_slice_in_dim(whole, first_row, slab_rows, 0)
        else:
            whole = gathered
            mine = current
        gram_matrix = lax.dot_general(
            whole, whole, (((1,), (1,)), ((), ())), preferred_element_type=jnp.float32
        ).astype(jnp.bfloat16)
        own_gram = lax.dynamic_slice_in_dim(gram_matrix, first_row, slab_rows, 0)
        polynomial = finish_rows(own_gram, gram_matrix)
        result = NEWTON_A * mine.astype(jnp.float32) + jnp.dot(
            polynomial, whole, preferred_element_type=jnp.float32
        )
        current = result.astype(jnp.bfloat16)
    return result


def on_device(grads, momentum, owner):
    slots = lax.axis_size("fsdp")
    replica = lax.axis_index("rep")
    width = grads.shape[-1]
    terms = grads[0].astype(jnp.float32)
    summed = lax.psum_scatter(terms, "rep", scatter_dimension=1, tiled=True)
    onehot = (owner[:, None] == jnp.arange(slots, dtype=jnp.int32)[None, :]).astype(jnp.float32)
    outgoing = jnp.einsum("es,eqd->sqd", onehot, summed, precision=lax.Precision.HIGHEST)
    arrived = lax.all_to_all(outgoing, "fsdp", split_axis=0, concat_axis=1, tiled=True)
    grad_rows = arrived[0]
    moment = momentum[0].reshape(-1, width)
    moment_new = DECAY_RATE * moment + grad_rows
    nesterov = (grad_rows + DECAY_RATE * moment_new).astype(jnp.bfloat16)
    slab_rows = nesterov.shape[0]
    first_row = replica * slab_rows
    result = rows_whole(nesterov, first_row)
    factor = math.sqrt(D)
    update_rows = (factor * result).astype(jnp.bfloat16)
    returning = lax.all_to_all(
        update_rows.reshape(slots, slab_rows // slots, width),
        "fsdp",
        split_axis=0,
        concat_axis=0,
        tiled=True,
    )
    updates = jnp.einsum(
        "es,sqd->eqd", onehot.astype(jnp.bfloat16), returning, preferred_element_type=jnp.float32
    ).astype(jnp.bfloat16)
    return (updates[:, None], moment_new.reshape(1, slots, slab_rows // slots, width))


def solution(mesh):
    placed = (P("rep", None, "fsdp", None), P("fsdp", None, "rep", None), P())
    return jax.shard_map(
        on_device,
        mesh=mesh,
        in_specs=placed,
        out_specs=(P(None, "fsdp", "rep", None), P("fsdp", None, "rep", None)),
        check_vma=False,
    )
```

profile of v0, /device:TPU:0, one launch (start us, length us, event | category | flops | bytes accessed | tf_op | source)
XLA Modules:
  0.0 329.2 jit_solution(4952600659564504718)
XLA Ops:
  7.2 0.0 reduce-scatter.2.cloned.1.call-start
  7.2 5.4 %bitcast_convert_fusion = f32[8,96,2048]{2,1,0:T(8,128)} fusion(bf16[1,8,96,2048]{3,2,1,0:T(8,128)(2,1)} %param.3), kind=kLoop, calls=%fused_computation.4 | loop fusion | flops 1572864 | bytes 9437184 | tf_op jit(solution)/shard_map/convert_element_type | solution.py:54
  12.6 0.0 reduce-scatter.2.cloned.1.call-update
  12.6 0.0 all-gather.3.cloned.1.call-start
  12.7 113.6 %reduce-scatter.2.cloned.1.call-done = f32[8,24,2048]{2,1,0:T(8,128)} async-done(((f32[8,96,2048]{2,1,0:T(8,128)}), f32[8,24,2048]{2,1,0:T(8,128)}) %reduce-scatter.2.cloned.1.call-update) | async-done | bytes 1572880 | tf_op jit(solution)/shard_map/reduce_scatter | solution.py:55
  126.3 0.0 copy-done.4
  126.3 3.1 fusion.9
  129.4 0.9 copy.21
  130.3 0.0 copy-start.2
  130.3 24.5 %all_to_all.14 = f32[8,24,2048]{2,1,0:T(8,128)S(1)} all-to-all(f32[8,24,2048]{2,1,0:T(8,128)S(1)} %copy.21), channel_id=1, replica_groups=mesh['rep'=4,'fsdp'=8] {'fsdp'}, dimensions={0} | all-to-all | bytes 3145728 | tf_op jit(solution)/shard_map/all_to_all | solution.py:58
  154.9 0.0 copy-done.2
  154.9 1.4 bitcast_add_fusion
  156.3 1.2 fusion.8
  157.4 0.0 all-gather.3.cloned.1.call-update
  157.5 0.2 all-gather.5.cloned.1.call-start
  157.7 62.1 %all-gather.3.cloned.1.call-done = bf16[768,2048]{1,0:T(8,128)(2,1)} async-done(((bf16[192,2048]{1,0:T(8,128)(2,1)}), bf16[768,2048]{1,0:T(8,128)(2,1)}) %all-gather.3.cloned.1.call-update) | async-done | bytes 3145744 | tf_op jit(solution)/shard_map/all_gather | solution.py:29
  219.8 4.3 %fusion = f32[]{:T(128)} fusion(bf16[768,2048]{1,0:T(8,128)(2,1)} %all-gather.3.cloned.1.call-done), kind=kLoop, calls=%fused_computation.2 | loop fusion | flops 4718591 | bytes 3145732 | tf_op jit(solution)/shard_map/reduce_sum | solution.py:32
  224.8 0.0 copy-done
  224.8 0.8 fusion.1
  225.6 0.0 copy-start.1
  225.6 1.6 copy-done.1
  227.2 2.6 convolution_convert_fusion.2
  229.9 4.0 %fusion.3 = bf16[192,2048]{1,0:T(8,128)(2,1)} fusion(bf16[768,2048]{1,0:T(8,128)(2,1)} %copy-done.1, bf16[768,768]{1,0:T(8,128)(2,1)S(1)} %convolution_convert_fusion.2, s32[]{:T(128)S(6)} %select_n.2), kind=kOutput, calls=%fused_computation.8 | convolution fusion | flops 832782336 | bytes 6489600 | tf_op jit(solution)/shard_map/dot_general | solution.py:43
  233.9 0.0 all-gather.5.cloned.1.call-update
  233.9 0.0 copy-start.3
  233.9 62.3 %all-gather.5.cloned.1.call-done = bf16[768,2048]{1,0:T(8,128)(2,1)} async-done(((bf16[192,2048]{1,0:T(8,128)(2,1)}), bf16[768,2048]{1,0:T(8,128)(2,1)}) %all-gather.5.cloned.1.call-update) | async-done | bytes 3145744 | tf_op jit(solution)/shard_map/all_gather | solution.py:29
  296.2 5.5 %convolution_convert_fusion.1 = bf16[768,768]{1,0:T(8,128)(2,1)S(1)} fusion(bf16[768,2048]{1,0:T(8,128)(2,1)} %all-gather.5.cloned.1.call-done), kind=kOutput, calls=%fused_computation.19 | convolution fusion | flops 2416508928 | bytes 4325376 | tf_op jit(solution)/shard_map/dot_general | solution.py:38
  301.7 0.0 copy-done.3
  301.7 3.0 fusion.4
  304.7 16.0 %all_to_all.15 = bf16[8,24,2048]{2,1,0:T(8,128)(2,1)S(1)} all-to-all(bf16[8,24,2048]{2,1,0:T(8,128)(2,1)S(1)} %bitcast.32), channel_id=1, replica_groups=mesh['rep'=4,'fsdp'=8] {'fsdp'}, dimensions={0} | all-to-all | bytes 1572864 | tf_op jit(solution)/shard_map/all_to_all | solution.py:68
  320.7 0.6 fusion.5
  321.3 1.3 copy.23
  (2 shorter events, 0.0 us)
Async XLA Ops:
  7.2 119.1 %reduce-scatter.2.cloned.1.call-start = ((), (), s32[]{:S(2)}) async-start(), calls=%async_computation.3 | async-start | bytes 7864320 | tf_op jit(solution)/shard_map/reduce_scatter | solution.py:55
  12.6 113.6 %copy-start.4 = (s32[8]{0:T(128)S(1)}, s32[8]{0:T(128)}, u32[]{:S(2)}) copy-start(s32[8]{0:T(128)} %param.5) | copy-start | bytes 100
  12.6 207.2 %all-gather.3.cloned.1.call-start = ((), (), s32[]{:S(2)}) async-start(), calls=%async_computation.4 | async-start | bytes 3932160 | tf_op jit(solution)/shard_map/all_gather | solution.py:29
  130.3 24.6 %copy-start.2 = (f32[1,8,24,2048]{3,2,1,0:T(8,128)S(1)}, f32[1,8,24,2048]{3,2,1,0:T(8,128)}, u32[]{:S(2)}) copy-start(f32[1,8,24,2048]{3,2,1,0:T(8,128)} %param.4) | copy-start | bytes 4718596
  157.5 138.8 %all-gather.5.cloned.1.call-start = ((), (), s32[]{:S(2)}) async-start(), calls=%async_computation.5 | async-start | bytes 3932160 | tf_op jit(solution)/shard_map/all_gather | solution.py:29
  219.8 5.0 %copy-start = (bf16[768,2048]{1,0:T(8,128)(2,1)S(1)}, bf16[768,2048]{1,0:T(8,128)(2,1)}, u32[]{:S(2)}) copy-start(bf16[768,2048]{1,0:T(8,128)(2,1)} %all-gather.3.cloned.1.call-done) | copy-start | bytes 9437188
  225.6 1.6 copy-start.1
  233.9 67.8 %copy-start.3 = (bf16[192,2048]{1,0:T(8,128)(2,1)S(1)}, bf16[192,2048]{1,0:T(8,128)(2,1)}, u32[]{:S(2)}) copy-start(bf16[192,2048]{1,0:T(8,128)(2,1)} %fusion.3) | copy-start | bytes 2359300
Sparse Core Ops, SparseCore 0:
  12.8 113.4 reduce-scatter.1
  157.6 62.2 all-gather.2
  234.0 62.1 all-gather.4
where the time goes:
time: 329 us
  waiting for transfers between devices  238 us (72%)
  blocking collectives  40.6 us (12%)
  matrix products  18.9 us (6%)
  between operations  14.5 us (4%)
  other arithmetic  13 us (4%)
  local copies, waits for them, and re-layouts  3.88 us (1%)
    all_gather x2, waiting for transfers between devices, rows_whole(): gathered = lax.all_gather(current, 'rep', axis=0, tiled=True)  124 us
    reduce_scatter x1, waiting for transfers between devices, on_device(): summed = lax.psum_scatter(terms, 'rep', scatter_dimension=1, tiled=True)  114 us
    all_to_all x1, blocking collectives, on_device(): lax.all_to_all(outgoing, 'fsdp', split_axis=0, concat_axis=1, tiled=True)  24.5 us
    all_to_all x1, blocking collectives, on_device(): lax.all_to_all(update_rows.reshape(slots, slab_rows // slots, width), 'fs...  16 us
    dot_general x2, matrix products, rows_whole(): lax.dot_general(whole, whole, (((1,), (1,)), ((), ())), preferred_element...  8.13 us
    dot_general x2, matrix products, rows_whole(): jnp.dot(polynomial, whole, preferred_element_type=jnp.float32)  6.98 us
  transfers between devices with their start and end apart: 3, of which 3 were waited for; matrix products, arithmetic and copies ran while one was open for 0% of the time, Pallas kernels for 0%

commit v1 on v0

--- a/solution.py
+++ b/solution.py
@@ -1,12 +1,15 @@
+import functools
 import math
 
 import jax
 import jax.numpy as jnp
 from jax import lax
+from jax.experimental import pallas as pl
+from jax.experimental.pallas import tpu as pltpu
 from jax.sharding import PartitionSpec as P
 
-D = 2048
 ITERS = 2
+CHUNKS = 4
 
 
 DECAY_RATE = 0.95
@@ -14,6 +17,352 @@
 NEWTON_B = -4.775
 NEWTON_C = 2.0315
 EPSILON = 1e-07
+MESH = pl.DeviceIdType.MESH
+F32 = jnp.float32
+BF16 = jnp.bfloat16
+
+
+def dot(left, right):
+    return jnp.dot(left, right, preferred_element_type=F32)
+
+
+def fold(block):
+    half = block.shape[1] // 2
+    return jnp.concatenate([block[:, :half], block[:, half:]], axis=0)
+
+
+def unfold(block):
+    half = block.shape[0] // 2
+    return jnp.concatenate([block[:half], block[half:]], axis=1)
+
+
+def step_kernel(
+    Z, F, C,
+    owner_ref, grads_ref, mom_ref,
+    upd_ref, mout_ref,
+    g32, sbuf, rbuf, asend, arecv, nall, gacc, gb, pb, g2b, wb, tsend,
+    rs_s, rs_r, a_s, a_r, ag_s, ag_r, t_s, t_r, *trecv,
+):
+    r = lax.axis_index("rep")
+    f = lax.axis_index("fsdp")
+    q, width = mom_ref.shape[2], mom_ref.shape[3]
+    cc = width // C
+    rows = F * q
+    ff = Z * rows
+    last = Z - 1
+
+    barrier = pltpu.get_barrier_semaphore()
+
+    @pl.when(r > 0)
+    def _():
+        pl.semaphore_signal(barrier, inc=1, device_id={"rep": r - 1}, device_id_type=MESH)
+
+    @pl.when(r < last)
+    def _():
+        pl.semaphore_signal(barrier, inc=1, device_id={"rep": r + 1}, device_id_type=MESH)
+
+    for k in range(1, F):
+        pl.semaphore_signal(barrier, inc=1, device_id={"fsdp": lax.rem(f + k, F)}, device_id_type=MESH)
+
+    owners = [owner_ref[e] for e in range(F)]
+    expert_of = []
+    for s in range(F):
+        found = jnp.int32(0)
+        for e in range(1, F):
+            found = jnp.where(owners[e] == s, jnp.int32(e), found)
+        expert_of.append(found)
+
+    def cols(c):
+        return pl.ds(c * cc, cc)
+
+    def prepare(c):
+        for s in range(F):
+            block = grads_ref[0, expert_of[s], :, cols(c)].astype(F32)
+            for d in range(Z):
+                g32[d, s * q:(s + 1) * q, cols(c)] = block[d * q:(d + 1) * q]
+
+    def position(way):
+        return r if way == 0 else last - r
+
+    def ahead(way, n):
+        return r + n if way == 0 else r - n
+
+    def rs_copy(c, way, t):
+        return pltpu.make_async_remote_copy(
+            src_ref=sbuf.at[way, c, t], dst_ref=rbuf.at[way, c, t],
+            send_sem=rs_s.at[way, c, t], recv_sem=rs_r.at[way, c, t],
+            device_id={"rep": ahead(way, 1)}, device_id_type=MESH)
+
+    def reduce_slot(c, t):
+        for way in range(2):
+            pos = position(way)
+            dest = ahead(way, last - t)
+            if t > 0:
+                @pl.when(jnp.logical_and(pos > 0, pos <= t))
+                def _(way=way, dest=dest):
+                    rs_copy(c, way, t - 1).wait_recv()
+                    sbuf[way, c, t] = (g32[dest, :, cols(c)] + rbuf[way, c, t - 1].astype(F32)).astype(BF16)
+                    rs_copy(c, way, t).start()
+
+            @pl.when(pos == 0)
+            def _(way=way, dest=dest):
+                sbuf[way, c, t] = g32[dest, :, cols(c)].astype(BF16)
+                rs_copy(c, way, t).start()
+
+    def a_copy(c, k):
+        peer = lax.rem(f + k, F)
+        return pltpu.make_async_remote_copy(
+            src_ref=asend.at[c, peer], dst_ref=arecv.at[c, f],
+            send_sem=a_s.at[c, k], recv_sem=a_r.at[c, k],
+            device_id={"fsdp": peer}, device_id_type=MESH)
+
+    def a_arrival(c, k):
+        peer = lax.rem(f + F - k, F)
+        return pltpu.make_async_remote_copy(
+            src_ref=asend.at[c, peer], dst_ref=arecv.at[c, peer],
+            send_sem=a_s.at[c, k], recv_sem=a_r.at[c, k],
+            device_id={"fsdp": peer}, device_id_type=MESH)
+
+    def reduce_last(c):
+        for way in range(2):
+            @pl.when(position(way) > 0)
+            def _(way=way):
+                rs_copy(c, way, last - 1).wait_recv()
+                g32[r, :, cols(c)] += rbuf[way, c, last - 1].astype(F32)
+        for s in range(F):
+            asend[c, s] = fold(g32[r, s * q:(s + 1) * q, cols(c)]).astype(BF16)
+        for k in range(1, F):
+            a_copy(c, k).start()
+        arecv[c, f] = asend[c, f]
+
+    def own_copy(c, way):
+        return pltpu.make_async_remote_copy(
+            src_ref=nall.at[c, r], dst_ref=nall.at[c, r],
+            send_sem=ag_s.at[way, c, 0], recv_sem=ag_r.at[way, c, 0],
+            device_id={"rep": ahead(way, 1)}, device_id_type=MESH)
+
+    def pass_copy(c, way, k):
+        source = ahead(way, -1 - k)
+        return pltpu.make_async_remote_copy(
+            src_ref=nall.at[c, source], dst_ref=nall.at[c, source],
+            send_sem=ag_s.at[way, c, k + 1], recv_sem=ag_r.at[way, c, k + 1],
+            device_id={"rep": ahead(way, 1)}, device_id_type=MESH)
+
+    def gather_arrival(c, way, k):
+        source = ahead(way, -1 - k)
+        return pltpu.make_async_remote_copy(
+            src_ref=nall.at[c, source], dst_ref=nall.at[c, source],
+            send_sem=ag_s.at[way, c, k], recv_sem=ag_r.at[way, c, k],
+            device_id={"rep": ahead(way, -1)}, device_id_type=MESH)
+
+    def momentum_rows(c):
+        for k in range(1, F):
+            a_arrival(c, k).wait_recv()
+        for pair in range(F // 2):
+            parts = []
+            for b in (2 * pair, 2 * pair + 1):
+                total = unfold(arecv[c, b].astype(F32))
+                moved = DECAY_RATE * mom_ref[0, b, :, cols(c)] + total
+                mout_ref[0, b, :, cols(c)] = moved
+                parts.append(total + DECAY_RATE * moved)
+            nall[c, r, 2 * pair * q:(2 * pair + 2) * q] = jnp.concatenate(parts, axis=0).astype(BF16)
+        for way in range(2):
+            @pl.when(position(way) < last)
+            def _(way=way):
+                own_copy(c, way).start()
+
+    def gather_slot(c, k):
+        for way in range(2):
+            pos = position(way)
+
+            @pl.when(pos > k)
+            def _(way=way):
+                gather_arrival(c, way, k).wait_recv()
+
+            if k + 1 < last:
+                @pl.when(jnp.logical_and(pos > k, pos < last))
+                def _(way=way):
+                    pass_copy(c, way, k).start()
+
+    def row_blocks(body):
+        size = ff // 2
+
+        def step(i, carry):
+            body(pl.ds(pl.multiple_of(i * size, size), size), i * size)
+            return carry
+
+        lax.fori_loop(0, 2, step, 0)
+
+    def gram(c):
+        whole = nall[c].reshape(ff, cc)
+        half = Z // 2
+
+        def step(i, carry):
+            mine = nall[c, pl.ds(i * half, half)].reshape(half * rows, cc)
+            part = lax.dot_general(mine, whole, (((1,), (1,)), ((), ())), preferred_element_type=F32)
+            at = pl.ds(pl.multiple_of(i * half * rows, half * rows), half * rows)
+            if c == 0:
+                gacc[at, :] = part
+            else:
+                gacc[at, :] += part
+            return carry
+
+        lax.fori_loop(0, 2, step, 0)
+
+    prepare(0)
+    pl.semaphore_wait(barrier, (F - 1) + (r > 0).astype(jnp.int32) + (r < last).astype(jnp.int32))
+    reduce_slot(0, 0)
+    for c in range(C):
+        if c + 1 < C:
+            prepare(c + 1)
+        for t in range(1, last):
+            reduce_slot(c, t)
+            if c > 0:
+                gather_slot(c - 1, t - 1)
+        if c + 1 < C:
+            reduce_slot(c + 1, 0)
+        reduce_last(c)
+        if c > 0:
+            gather_slot(c - 1, last - 1)
+            gram(c - 1)
+        momentum_rows(c)
+    for k in range(last):
+        gather_slot(C - 1, k)
+    gram(C - 1)
+
+    trace = jnp.zeros((1, 1), F32)
+    size = ff // 2
+    for i in range(2):
+        at = slice(i * size, (i + 1) * size)
+        row = lax.broadcasted_iota(jnp.int32, (size, size), 0)
+        col = lax.broadcasted_iota(jnp.int32, (size, size), 1)
+        trace += jnp.sum(jnp.where(row == col, gacc[at, at], 0.0), keepdims=True)
+    scale = 1.0 / (jnp.sqrt(trace) + EPSILON)
+
+    def normalise(at, _):
+        scaled = gacc[at, :] * (scale * scale)
+        gacc[at, :] = scaled
+        gb[at, :] = scaled.astype(BF16)
+
+    row_blocks(normalise)
+
+    def first_polynomial(at, _):
+        mine = gb[at, :]
+        pb[at, :] = (NEWTON_B * mine.astype(F32) + NEWTON_C * dot(mine, gb[...])).astype(BF16)
+
+    row_blocks(first_polynomial)
+
+    def second_gram(at, _):
+        mixed = dot(pb[at, :], gb[...])
+        outer = dot(mixed.astype(BF16), pb[...])
+        g2b[at, :] = (NEWTON_A * NEWTON_A * gacc[at, :] + 2.0 * NEWTON_A * mixed + outer).astype(BF16)
+
+    row_blocks(second_gram)
+
+    own = pl.ds(pl.multiple_of(r * rows, rows), rows)
+    mine = g2b[own, :]
+    second = (NEWTON_B * mine.astype(F32) + NEWTON_C * dot(mine, g2b[...])).astype(BF16)
+    wb[...] = (
+        NEWTON_A * (second.astype(F32) + pb[own, :].astype(F32)) + dot(second, pb[...])
+    ).astype(BF16)
+
+    def t_copy(c, k):
+        peer = lax.rem(f + k, F)
+        return pltpu.make_async_remote_copy(
+            src_ref=tsend.at[c, peer], dst_ref=trecv[c].at[f],
+            send_sem=t_s.at[c, k], recv_sem=t_r.at[c, k],
+            device_id={"fsdp": peer}, device_id_type=MESH)
+
+    def t_arrival(c, k):
+        peer = lax.rem(f + F - k, F)
+        return pltpu.make_async_remote_copy(
+            src_ref=tsend.at[c, peer], dst_ref=trecv[c].at[peer],
+            send_sem=t_s.at[c, k], recv_sem=t_r.at[c, k],
+            device_id={"fsdp": peer}, device_id_type=MESH)
+
+    factor = scale * math.sqrt(width)
+    for c in range(C):
+        product = dot(wb[...], nall[c].reshape(ff, cc))
+        result = factor * (NEWTON_A * NEWTON_A * nall[c, r].astype(F32) + product)
+        for b in range(F):
+            tsend[c, b] = fold(result[b * q:(b + 1) * q]).astype(BF16)
+        for k in range(1, F):
+            t_copy(c, k).start()
+        trecv[c][f] = tsend[c, f]
+
+    for c in range(C):
+        for k in range(1, F):
+            t_arrival(c, k).wait_recv()
+        for e in range(F):
+            upd_ref[e, 0, :, cols(c)] = unfold(trecv[c][owners[e]].astype(F32)).astype(BF16)
+
+    for c in range(C):
+        for way in range(2):
+            pos = position(way)
+            for t in range(last):
+                @pl.when(pos <= t)
+                def _(c=c, way=way, t=t):
+                    rs_copy(c, way, t).wait_send()
+
+            @pl.when(pos < last)
+            def _(c=c, way=way):
+                own_copy(c, way).wait_send()
+
+            for k in range(last - 1):
+                @pl.when(jnp.logical_and(pos > k, pos < last))
+                def _(c=c, way=way, k=k):
+                    pass_copy(c, way, k).wait_send()
+        for k in range(1, F):
+            a_copy(c, k).wait_send()
+            t_copy(c, k).wait_send()
+
+
+def fused_step(grads, momentum, owner):
+    Z, F = lax.axis_size("rep"), lax.axis_size("fsdp")
+    q, width = momentum.shape[2], momentum.shape[3]
+    C = CHUNKS
+    cc = width // C
+    rows = F * q
+    ff = Z * rows
+    vmem = pl.BlockSpec(memory_space=pltpu.VMEM)
+    dma = pltpu.SemaphoreType.DMA
+    return pl.pallas_call(
+        functools.partial(step_kernel, Z, F, C),
+        out_shape=(
+            jax.ShapeDtypeStruct((F, 1, q, width), BF16),
+            jax.ShapeDtypeStruct(momentum.shape, F32),
+        ),
+        in_specs=[pl.BlockSpec(memory_space=pltpu.SMEM), vmem, vmem],
+        out_specs=(vmem, vmem),
+        scratch_shapes=[
+            pltpu.VMEM((Z, rows, width), F32),
+            pltpu.VMEM((2, C, Z - 1, rows, cc), BF16),
+            pltpu.VMEM((2, C, Z - 1, rows, cc), BF16),
+            pltpu.VMEM((C, F, 2 * q, cc // 2), BF16),
+            pltpu.VMEM((C, F, 2 * q, cc // 2), BF16),
+            pltpu.VMEM((C, Z, rows, cc), BF16),
+            pltpu.VMEM((ff, ff), F32),
+            pltpu.VMEM((ff, ff), BF16),
+            pltpu.VMEM((ff, ff), BF16),
+            pltpu.VMEM((ff, ff), BF16),
+            pltpu.VMEM((rows, ff), BF16),
+            pltpu.VMEM((C, F, 2 * q, cc // 2), BF16),
+            dma((2, C, Z - 1)),
+            dma((2, C, Z - 1)),
+            dma((C, F)),
+            dma((C, F)),
+            dma((2, C, Z - 1)),
+            dma((2, C, Z - 1)),
+            dma((C, F)),
+            dma((C, F)),
+        ] + [pltpu.VMEM((F, 2 * q, cc // 2), BF16)] * C,
+        compiler_params=pltpu.CompilerParams(
+            collective_id=0, has_side_effects=True, vmem_limit_bytes=58 * 1024 * 1024
+        ),
+        cost_estimate=pl.CostEstimate(
+            flops=2 * ff * ff * width, bytes_accessed=16 * rows * width, transcendentals=0
+        ),
+    )(owner, grads, momentum)
 
 
 def finish_rows(own_gram, gram_matrix):
@@ -63,7 +412,7 @@
     slab_rows = nesterov.shape[0]
     first_row = replica * slab_rows
     result = rows_whole(nesterov, first_row)
-    factor = math.sqrt(D)
+    factor = math.sqrt(width)
     update_rows = (factor * result).astype(jnp.bfloat16)
     returning = lax.all_to_all(
         update_rows.reshape(slots, slab_rows // slots, width),
@@ -78,10 +427,18 @@
     return (updates[:, None], moment_new.reshape(1, slots, slab_rows // slots, width))
 
 
+def step(grads, momentum, owner):
+    Z, F = lax.axis_size("rep"), lax.axis_size("fsdp")
+    q, width = momentum.shape[2], momentum.shape[3]
+    if q % 8 == 0 and F % 2 == 0 and Z % 2 == 0 and Z > 2 and width % (256 * CHUNKS) == 0:
+        return fused_step(grads, momentum, owner)
+    return on_device(grads, momentum, owner)
+
+
 def solution(mesh):
     placed = (P("rep", None, "fsdp", None), P("fsdp", None, "rep", None), P())
     return jax.shard_map(
-        on_device,
+        step,
         mesh=mesh,
         in_specs=placed,
         out_specs=(P(None, "fsdp", "rep", None), P("fsdp", None, "rep", None)),

time: 329 us -> 134 us (0.41)
  waiting for transfers between devices: 238 us -> 0 us
  Pallas kernels: 0 us -> 130 us
  blocking collectives: 40.6 us -> 0 us
  matrix products: 18.9 us -> 0 us
  between operations: 14.5 us -> 0.65 us
  other arithmetic: 13 us -> 0 us
    pallas_call x0 -> x1, Pallas kernels: none -> 130 us  [fused_step(): pl.pallas_call(functools.partial(step_kernel, Z, F, C), out_shape=(jax.Sh...]
    all_gather x2 -> x0, waiting for transfers between devices: 124 us -> none  [rows_whole(): gathered = lax.all_gather(current, 'rep', axis=0, tiled=True)]
    reduce_scatter x1 -> x0, waiting for transfers between devices: 114 us -> none  [on_device(): summed = lax.psum_scatter(terms, 'rep', scatter_dimension=1, tiled=True)]
    all_to_all x2 -> x0, blocking collectives: 40.6 us -> none  [the longest x1 24.5 us: on_device(): lax.all_to_all(outgoing, 'fsdp', split_axis=0, concat_axis=1, tiled=True)]
    dot_general x6 -> x0, matrix products: 18.9 us -> none  [the longest x2 8.13 us: rows_whole(): lax.dot_general(whole, whole, (((1,), (1,)), ((), ())), preferred_element...]
    convert_element_type x3 -> x0, other arithmetic: 7.32 us -> none  [the longest x1 5.4 us: on_device(): terms = grads[0].astype(jnp.float32)]
    reduce_sum x1 -> x0, other arithmetic: 4.26 us -> none  [rows_whole(): frobenius = jnp.sqrt(jnp.sum(values * values))]
  transfers between devices with their start and end apart: 3 -> 0, of which waited for: 3 -> 0; matrix products, arithmetic and copies ran while one was open for 0% -> 0% of each run, Pallas kernels for 0% -> 0%
where the time goes in v1:
time: 134 us
  Pallas kernels  130 us (97%)
  local copies, waits for them, and re-layouts  3.35 us (2%)
    pallas_call x1, Pallas kernels, fused_step(): pl.pallas_call(functools.partial(step_kernel, Z, F, C), out_shape=(jax.Sh...  130 us
    unnamed x4, local copies, waits for them, and re-layouts  3.35 us

profile of v1, /device:TPU:0, one launch (start us, length us, event | category | flops | bytes accessed | tf_op | source)
XLA Modules:
  0.0 133.9 jit_solution(7722939253968771739)
XLA Ops:
  0.6 129.9 %shard_map.50 = (bf16[8,1,24,2048]{3,2,1,0:T(8,128)(2,1)}, f32[1,8,24,2048]{3,2,1,0:T(8,128)}) custom-call(s32[8]{0:T(128)} %owner_ref.1, bf16[1,8,96,2048]{3,2,1,0:T(8,128)(2,1)} %grads_ref.1, f32[1,8,24,2048]{3,2,1,0:T(8,128)} %mom_ref.1), custom_call_target="tpu_custom_call" | custom-call | flops 2415919104 | bytes 6291456 | tf_op jit(solution)/shard_map/pallas_call | solution.py:329
  130.6 0.0 copy-start
  130.6 2.2 %copy.7 = bf16[8,1,24,2048]{3,2,1,0:T(8,128)(2,1)} copy(bf16[8,1,24,2048]{3,2,1,0:T(8,128)(2,1)} %get-tuple-element.4) | data formatting | bytes 1572864
  132.8 0.0 copy-done
  132.8 1.1 copy.8
Async XLA Ops:
  130.6 2.2 %copy-start = (f32[1,8,24,2048]{3,2,1,0:T(8,128)S(1)}, f32[1,8,24,2048]{3,2,1,0:T(8,128)}, u32[]{:S(2)}) copy-start(f32[1,8,24,2048]{3,2,1,0:T(8,128)} %get-tuple-element.5) | copy-start | bytes 4718596

commit v2 on v1

--- a/solution.py
+++ b/solution.py
@@ -9,7 +9,7 @@
 from jax.sharding import PartitionSpec as P
 
 ITERS = 2
-CHUNKS = 4
+CHUNKS = 8
 
 
 DECAY_RATE = 0.95
@@ -34,6 +34,18 @@
 def unfold(block):
     half = block.shape[0] // 2
     return jnp.concatenate([block[:half], block[half:]], axis=1)
+
+
+def schedule(Z, C):
+    start, stride, exchange = 0.34, 0.65, 0.57
+    stages = [(0.0, "prepare", 0)]
+    stages += [(start + stride * t, "reduce", t) for t in range(Z - 1)]
+    owner = start + stride * (Z - 1)
+    stages += [(owner, "owner", 0), (owner + exchange, "momentum", 0)]
+    stages += [(owner + exchange + stride * (k + 1), "gather", k) for k in range(Z - 1)]
+    stages += [(owner + exchange + stride * (Z - 1) + 0.1, "gram", 0)]
+    order = sorted((c + at, stage, c, n) for c in range(C) for at, stage, n in stages)
+    return [item[1:] for item in order]
 
 
 def step_kernel(
@@ -211,24 +223,19 @@
 
     prepare(0)
     pl.semaphore_wait(barrier, (F - 1) + (r > 0).astype(jnp.int32) + (r < last).astype(jnp.int32))
-    reduce_slot(0, 0)
-    for c in range(C):
-        if c + 1 < C:
-            prepare(c + 1)
-        for t in range(1, last):
-            reduce_slot(c, t)
-            if c > 0:
-                gather_slot(c - 1, t - 1)
-        if c + 1 < C:
-            reduce_slot(c + 1, 0)
-        reduce_last(c)
-        if c > 0:
-            gather_slot(c - 1, last - 1)
-            gram(c - 1)
-        momentum_rows(c)
-    for k in range(last):
-        gather_slot(C - 1, k)
-    gram(C - 1)
+    for stage, c, n in schedule(Z, C):
+        if stage == "prepare" and c > 0:
+            prepare(c)
+        elif stage == "reduce":
+            reduce_slot(c, n)
+        elif stage == "owner":
+            reduce_last(c)
+        elif stage == "momentum":
+            momentum_rows(c)
+        elif stage == "gather":
+            gather_slot(c, n)
+        elif stage == "gram":
+            gram(c)
 
     trace = jnp.zeros((1, 1), F32)
     size = ff // 2

time: 134 us -> 116 us (0.87)
  Pallas kernels: 130 us -> 112 us
    pallas_call x1, Pallas kernels: 130 us -> 112 us  [fused_step(): pl.pallas_call(functools.partial(step_kernel, Z, F, C), out_shape=(jax.Sh...]
where the time goes in v2:
time: 116 us
  Pallas kernels  112 us (97%)
  local copies, waits for them, and re-layouts  3.35 us (3%)
    pallas_call x1, Pallas kernels, fused_step(): pl.pallas_call(functools.partial(step_kernel, Z, F, C), out_shape=(jax.Sh...  112 us
    unnamed x4, local copies, waits for them, and re-layouts  3.35 us

profile of v2, /device:TPU:0, one launch (start us, length us, event | category | flops | bytes accessed | tf_op | source)
XLA Modules:
  0.0 115.9 jit_solution(15534017424085729432)
XLA Ops:
  0.6 111.9 %shard_map.50 = (bf16[8,1,24,2048]{3,2,1,0:T(8,128)(2,1)}, f32[1,8,24,2048]{3,2,1,0:T(8,128)}) custom-call(s32[8]{0:T(128)} %owner_ref.1, bf16[1,8,96,2048]{3,2,1,0:T(8,128)(2,1)} %grads_ref.1, f32[1,8,24,2048]{3,2,1,0:T(8,128)} %mom_ref.1), custom_call_target="tpu_custom_call" | custom-call | flops 2415919104 | bytes 6291456 | tf_op jit(solution)/shard_map/pallas_call | solution.py:336
  112.5 0.0 copy-start
  112.5 2.2 %copy.7 = bf16[8,1,24,2048]{3,2,1,0:T(8,128)(2,1)} copy(bf16[8,1,24,2048]{3,2,1,0:T(8,128)(2,1)} %get-tuple-element.4) | data formatting | bytes 1572864
  114.7 0.0 copy-done
  114.7 1.1 copy.8
Async XLA Ops:
  112.5 2.2 %copy-start = (f32[1,8,24,2048]{3,2,1,0:T(8,128)S(1)}, f32[1,8,24,2048]{3,2,1,0:T(8,128)}, u32[]{:S(2)}) copy-start(f32[1,8,24,2048]{3,2,1,0:T(8,128)} %get-tuple-element.5) | copy-start | bytes 4718596

commit v3 on v2

--- a/solution.py
+++ b/solution.py
@@ -37,7 +37,7 @@
 
 
 def schedule(Z, C):
-    start, stride, exchange = 0.34, 0.65, 0.57
+    start, stride, exchange = 0.34, 0.8, 0.5
     stages = [(0.0, "prepare", 0)]
     stages += [(start + stride * t, "reduce", t) for t in range(Z - 1)]
     owner = start + stride * (Z - 1)
@@ -50,11 +50,12 @@
 
 def step_kernel(
     Z, F, C,
-    owner_ref, grads_ref, mom_ref,
-    upd_ref, mout_ref,
+    owner_ref, grads_hbm, mom_hbm,
+    upd_ref, total_ref,
     g32, sbuf, rbuf, asend, arecv, nall, gacc, gb, pb, g2b, wb, tsend,
-    rs_s, rs_r, a_s, a_r, ag_s, ag_r, t_s, t_r, *trecv,
+    rs_s, rs_r, a_s, a_r, ag_s, ag_r, t_s, t_r, mom_ref, load_sem, *split,
 ):
+    trecv, loaded = split[:C], split[C:]
     r = lax.axis_index("rep")
     f = lax.axis_index("fsdp")
     q, width = mom_ref.shape[2], mom_ref.shape[3]
@@ -63,6 +64,15 @@
     ff = Z * rows
     last = Z - 1
 
+    def load(c):
+        return pltpu.make_async_copy(
+            grads_hbm.at[0, :, :, pl.ds(c * cc, cc)], loaded[c], load_sem.at[c])
+
+    mom_load = pltpu.make_async_copy(mom_hbm, mom_ref, load_sem.at[C])
+    for c in range(C):
+        load(c).start()
+    mom_load.start()
+
     barrier = pltpu.get_barrier_semaphore()
 
     @pl.when(r > 0)
@@ -88,8 +98,9 @@
         return pl.ds(c * cc, cc)
 
     def prepare(c):
+        load(c).wait()
         for s in range(F):
-            block = grads_ref[0, expert_of[s], :, cols(c)].astype(F32)
+            block = loaded[c][expert_of[s]].astype(F32)
             for d in range(Z):
                 g32[d, s * q:(s + 1) * q, cols(c)] = block[d * q:(d + 1) * q]
 
@@ -168,6 +179,8 @@
             device_id={"rep": ahead(way, -1)}, device_id_type=MESH)
 
     def momentum_rows(c):
+        if c == 0:
+            mom_load.wait()
         for k in range(1, F):
             a_arrival(c, k).wait_recv()
         for pair in range(F // 2):
@@ -175,7 +188,7 @@
             for b in (2 * pair, 2 * pair + 1):
                 total = unfold(arecv[c, b].astype(F32))
                 moved = DECAY_RATE * mom_ref[0, b, :, cols(c)] + total
-                mout_ref[0, b, :, cols(c)] = moved
+                total_ref[0, b, :, cols(c)] = total.astype(BF16)
                 parts.append(total + DECAY_RATE * moved)
             nall[c, r, 2 * pair * q:(2 * pair + 2) * q] = jnp.concatenate(parts, axis=0).astype(BF16)
         for way in range(2):
@@ -206,12 +219,18 @@
         lax.fori_loop(0, 2, step, 0)
 
     def gram(c):
-        whole = nall[c].reshape(ff, cc)
+        if c % 2 == 1 and c < C - 1:
+            return
+        group = [c] if c in (0, C - 1) else [c - 1, c]
         half = Z // 2
 
         def step(i, carry):
-            mine = nall[c, pl.ds(i * half, half)].reshape(half * rows, cc)
-            part = lax.dot_general(mine, whole, (((1,), (1,)), ((), ())), preferred_element_type=F32)
+            part = None
+            for g in group:
+                mine = nall[g, pl.ds(i * half, half)].reshape(half * rows, cc)
+                term = lax.dot_general(
+                    mine, nall[g].reshape(ff, cc), (((1,), (1,)), ((), ())), preferred_element_type=F32)
+                part = term if part is None else part + term
             at = pl.ds(pl.multiple_of(i * half * rows, half * rows), half * rows)
             if c == 0:
                 gacc[at, :] = part
@@ -333,13 +352,14 @@
     ff = Z * rows
     vmem = pl.BlockSpec(memory_space=pltpu.VMEM)
     dma = pltpu.SemaphoreType.DMA
-    return pl.pallas_call(
+    any_place = pl.BlockSpec(memory_space=pl.ANY)
+    updates, total = pl.pallas_call(
         functools.partial(step_kernel, Z, F, C),
         out_shape=(
             jax.ShapeDtypeStruct((F, 1, q, width), BF16),
-            jax.ShapeDtypeStruct(momentum.shape, F32),
+            jax.ShapeDtypeStruct(momentum.shape, BF16),
         ),
-        in_specs=[pl.BlockSpec(memory_space=pltpu.SMEM), vmem, vmem],
+        in_specs=[pl.BlockSpec(memory_space=pltpu.SMEM), any_place, any_place],
         out_specs=(vmem, vmem),
         scratch_shapes=[
             pltpu.VMEM((Z, rows, width), F32),
@@ -362,7 +382,11 @@
             dma((2, C, Z - 1)),
             dma((C, F)),
             dma((C, F)),
-        ] + [pltpu.VMEM((F, 2 * q, cc // 2), BF16)] * C,
+            pltpu.VMEM(momentum.shape, F32),
+            dma((C + 1,)),
+        ]
+        + [pltpu.VMEM((F, 2 * q, cc // 2), BF16)] * C
+        + [pltpu.VMEM(grads.shape[1:3] + (cc,), BF16)] * C,
         compiler_params=pltpu.CompilerParams(
             collective_id=0, has_side_effects=True, vmem_limit_bytes=58 * 1024 * 1024
         ),
@@ -370,6 +394,7 @@
             flops=2 * ff * ff * width, bytes_accessed=16 * rows * width, transcendentals=0
         ),
     )(owner, grads, momentum)
+    return updates, DECAY_RATE * momentum + total.astype(F32)
 
 
 def finish_rows(own_gram, gram_matrix):

time: 116 us -> 113 us (0.974)
  Pallas kernels: 112 us -> 108 us
  other arithmetic: 0 us -> 2.6 us
  local copies, waits for them, and re-layouts: 3.35 us -> 0.89 us
    pallas_call x1, Pallas kernels: 112 us -> 108 us  [fused_step(): pl.pallas_call(functools.partial(step_kernel, Z, F, C), out_shape=(jax.Sh...]
    add x0 -> x1, other arithmetic: none -> 2.6 us  [fused_step(): return (updates, DECAY_RATE * momentum + total.astype(F32))]
    unnamed x4 -> x5, local copies, waits for them, and re-layouts: 3.35 us -> 0.89 us
where the time goes in v3:
time: 113 us; the launch traced here: 112 us
  Pallas kernels  108 us (96%)
  other arithmetic  2.6 us (2%)
    pallas_call x1, Pallas kernels, fused_step(): pl.pallas_call(functools.partial(step_kernel, Z, F, C), out_shape=(jax.Sh...  108 us
    add x1, other arithmetic, fused_step(): return (updates, DECAY_RATE * momentum + total.astype(F32))  2.6 us

profile of v3, /device:TPU:0, one launch (start us, length us, event | category | flops | bytes accessed | tf_op | source)
XLA Modules:
  0.0 112.4 jit_solution(15991381657884610845)
XLA Ops:
  0.6 0.0 copy-start
  0.6 108.2 %shard_map.50 = (bf16[8,1,24,2048]{3,2,1,0:T(8,128)(2,1)}, bf16[1,8,24,2048]{3,2,1,0:T(8,128)(2,1)}) custom-call(s32[8]{0:T(128)} %owner_ref.1, bf16[1,8,96,2048]{3,2,1,0:T(8,128)(2,1)} %grads_hbm.1, f32[1,8,24,2048]{3,2,1,0:T(8,128)} %mom_hbm.1), custom_call_target="tpu_custom_call" | custom-call | flops 2415919104 | bytes 6291456 | tf_op jit(solution)/shard_map/pallas_call | solution.py:356
  108.9 0.0 copy-done
  108.9 0.0 copy-start.1
  108.9 2.6 %convert_add_fusion = f32[1,8,24,2048]{3,2,1,0:T(8,128)} fusion(bf16[1,8,24,2048]{3,2,1,0:T(8,128)(2,1)} %get-tuple-element.5, f32[1,8,24,2048]{3,2,1,0:T(8,128)S(1)} %copy-done), kind=kLoop, calls=%fused_computation | loop fusion | flops 1179648 | bytes 3932160 | tf_op jit(solution)/shard_map/add | solution.py:397
  111.5 0.0 copy-done.1
  111.5 0.9 copy.6
Async XLA Ops:
  0.6 108.2 %copy-start = (f32[1,8,24,2048]{3,2,1,0:T(8,128)S(1)}, f32[1,8,24,2048]{3,2,1,0:T(8,128)}, u32[]{:S(2)}) copy-start(f32[1,8,24,2048]{3,2,1,0:T(8,128)} %mom_hbm.1) | copy-start | bytes 4718596
  108.9 2.6 %copy-start.1 = (bf16[8,1,24,2048]{3,2,1,0:T(8,128)(2,1)S(1)}, bf16[8,1,24,2048]{3,2,1,0:T(8,128)(2,1)}, u32[]{:S(2)}) copy-start(bf16[8,1,24,2048]{3,2,1,0:T(8,128)(2,1)} %get-tuple-element.8) | copy-start | bytes 2359300

commit v4 on v3

--- a/solution.py
+++ b/solution.py
@@ -55,7 +55,7 @@
     g32, sbuf, rbuf, asend, arecv, nall, gacc, gb, pb, g2b, wb, tsend,
     rs_s, rs_r, a_s, a_r, ag_s, ag_r, t_s, t_r, mom_ref, load_sem, *split,
 ):
-    trecv, loaded = split[:C], split[C:]
+    trecv, loaded = split[:C // 2], split[C // 2:]
     r = lax.axis_index("rep")
     f = lax.axis_index("fsdp")
     q, width = mom_ref.shape[2], mom_ref.shape[3]
@@ -152,11 +152,11 @@
             def _(way=way):
                 rs_copy(c, way, last - 1).wait_recv()
                 g32[r, :, cols(c)] += rbuf[way, c, last - 1].astype(F32)
-        for s in range(F):
-            asend[c, s] = fold(g32[r, s * q:(s + 1) * q, cols(c)]).astype(BF16)
-        for k in range(1, F):
+        for k in range(1, F):
+            peer = lax.rem(f + k, F)
+            asend[c, peer] = fold(g32[r, pl.ds(pl.multiple_of(peer * q, q), q), cols(c)]).astype(BF16)
             a_copy(c, k).start()
-        arecv[c, f] = asend[c, f]
+        arecv[c, f] = fold(g32[r, pl.ds(pl.multiple_of(f * q, q), q), cols(c)]).astype(BF16)
 
     def own_copy(c, way):
         return pltpu.make_async_remote_copy(
@@ -266,9 +266,7 @@
     scale = 1.0 / (jnp.sqrt(trace) + EPSILON)
 
     def normalise(at, _):
-        scaled = gacc[at, :] * (scale * scale)
-        gacc[at, :] = scaled
-        gb[at, :] = scaled.astype(BF16)
+        gb[at, :] = (gacc[at, :] * (scale * scale)).astype(BF16)
 
     row_blocks(normalise)
 
@@ -281,7 +279,7 @@
     def second_gram(at, _):
         mixed = dot(pb[at, :], gb[...])
         outer = dot(mixed.astype(BF16), pb[...])
-        g2b[at, :] = (NEWTON_A * NEWTON_A * gacc[at, :] + 2.0 * NEWTON_A * mixed + outer).astype(BF16)
+        g2b[at, :] = (NEWTON_A * NEWTON_A * (gacc[at, :] * (scale * scale)) + 2.0 * NEWTON_A * mixed + outer).astype(BF16)
 
     row_blocks(second_gram)
 
@@ -307,20 +305,22 @@
             device_id={"fsdp": peer}, device_id_type=MESH)
 
     factor = scale * math.sqrt(width)
-    for c in range(C):
-        product = dot(wb[...], nall[c].reshape(ff, cc))
-        result = factor * (NEWTON_A * NEWTON_A * nall[c, r].astype(F32) + product)
+    for g in range(C // 2):
+        halves = []
+        for c in (2 * g, 2 * g + 1):
+            product = dot(wb[...], nall[c].reshape(ff, cc))
+            halves.append(factor * (NEWTON_A * NEWTON_A * nall[c, r].astype(F32) + product))
         for b in range(F):
-            tsend[c, b] = fold(result[b * q:(b + 1) * q]).astype(BF16)
-        for k in range(1, F):
-            t_copy(c, k).start()
-        trecv[c][f] = tsend[c, f]
-
-    for c in range(C):
-        for k in range(1, F):
-            t_arrival(c, k).wait_recv()
+            tsend[g, b] = jnp.concatenate([half[b * q:(b + 1) * q] for half in halves], axis=0).astype(BF16)
+        for k in range(1, F):
+            t_copy(g, k).start()
+        trecv[g][f] = tsend[g, f]
+
+    for g in range(C // 2):
+        for k in range(1, F):
+            t_arrival(g, k).wait_recv()
         for e in range(F):
-            upd_ref[e, 0, :, cols(c)] = unfold(trecv[c][owners[e]].astype(F32)).astype(BF16)
+            upd_ref[e, 0, :, pl.ds(2 * g * cc, 2 * cc)] = unfold(trecv[g][owners[e]].astype(F32)).astype(BF16)
 
     for c in range(C):
         for way in range(2):
@@ -340,7 +340,9 @@
                     pass_copy(c, way, k).wait_send()
         for k in range(1, F):
             a_copy(c, k).wait_send()
-            t_copy(c, k).wait_send()
+    for g in range(C // 2):
+        for k in range(1, F):
+            t_copy(g, k).wait_send()
 
 
 def fused_step(grads, momentum, owner):
@@ -373,7 +375,7 @@
             pltpu.VMEM((ff, ff), BF16),
             pltpu.VMEM((ff, ff), BF16),
             pltpu.VMEM((rows, ff), BF16),
-            pltpu.VMEM((C, F, 2 * q, cc // 2), BF16),
+            pltpu.VMEM((C // 2, F, 2 * q, cc), BF16),
             dma((2, C, Z - 1)),
             dma((2, C, Z - 1)),
             dma((C, F)),
@@ -385,7 +387,7 @@
             pltpu.VMEM(momentum.shape, F32),
             dma((C + 1,)),
         ]
-        + [pltpu.VMEM((F, 2 * q, cc // 2), BF16)] * C
+        + [pltpu.VMEM((F, 2 * q, cc), BF16)] * (C // 2)
         + [pltpu.VMEM(grads.shape[1:3] + (cc,), BF16)] * C,
         compiler_params=pltpu.CompilerParams(
             collective_id=0, has_side_effects=True, vmem_limit_bytes=58 * 1024 * 1024

time: 113 us -> 112 us (level)
  no operation moved by 1% of the time
where the time goes in v4:
time: 112 us
  Pallas kernels  108 us (96%)
  other arithmetic  2.6 us (2%)
    pallas_call x1, Pallas kernels, fused_step(): pl.pallas_call(functools.partial(step_kernel, Z, F, C), out_shape=(jax.Sh...  108 us
    add x1, other arithmetic, fused_step(): return (updates, DECAY_RATE * momentum + total.astype(F32))  2.6 us

profile of v4, /device:TPU:0, one launch (start us, length us, event | category | flops | bytes accessed | tf_op | source)
XLA Modules:
  0.0 112.0 jit_solution(12809772871619208120)
XLA Ops:
  0.6 0.0 copy-start
  0.6 107.8 %shard_map.50 = (bf16[8,1,24,2048]{3,2,1,0:T(8,128)(2,1)}, bf16[1,8,24,2048]{3,2,1,0:T(8,128)(2,1)}) custom-call(s32[8]{0:T(128)} %owner_ref.1, bf16[1,8,96,2048]{3,2,1,0:T(8,128)(2,1)} %grads_hbm.1, f32[1,8,24,2048]{3,2,1,0:T(8,128)} %mom_hbm.1), custom_call_target="tpu_custom_call" | custom-call | flops 2415919104 | bytes 6291456 | tf_op jit(solution)/shard_map/pallas_call | solution.py:358
  108.4 0.0 copy-done
  108.5 0.0 copy-start.1
  108.5 2.6 %convert_add_fusion = f32[1,8,24,2048]{3,2,1,0:T(8,128)} fusion(bf16[1,8,24,2048]{3,2,1,0:T(8,128)(2,1)} %get-tuple-element.5, f32[1,8,24,2048]{3,2,1,0:T(8,128)S(1)} %copy-done), kind=kLoop, calls=%fused_computation | loop fusion | flops 1179648 | bytes 3932160 | tf_op jit(solution)/shard_map/add | solution.py:399
  111.1 0.0 copy-done.1
  111.1 0.9 copy.6
Async XLA Ops:
  0.6 107.8 %copy-start = (f32[1,8,24,2048]{3,2,1,0:T(8,128)S(1)}, f32[1,8,24,2048]{3,2,1,0:T(8,128)}, u32[]{:S(2)}) copy-start(f32[1,8,24,2048]{3,2,1,0:T(8,128)} %mom_hbm.1) | copy-start | bytes 4718596
  108.5 2.6 %copy-start.1 = (bf16[8,1,24,2048]{3,2,1,0:T(8,128)(2,1)S(1)}, bf16[8,1,24,2048]{3,2,1,0:T(8,128)(2,1)}, u32[]{:S(2)}) copy-start(bf16[8,1,24,2048]{3,2,1,0:T(8,128)(2,1)} %get-tuple-element.8) | copy-start | bytes 2359300

commit v5 on v3

--- a/solution.py
+++ b/solution.py
@@ -43,7 +43,7 @@
     owner = start + stride * (Z - 1)
     stages += [(owner, "owner", 0), (owner + exchange, "momentum", 0)]
     stages += [(owner + exchange + stride * (k + 1), "gather", k) for k in range(Z - 1)]
-    stages += [(owner + exchange + stride * (Z - 1) + 0.1, "gram", 0)]
+    stages += [(owner + exchange + stride * (Z - 1) + 0.33, "gram", 0)]
     order = sorted((c + at, stage, c, n) for c in range(C) for at, stage, n in stages)
     return [item[1:] for item in order]
 

time: 113 us -> 113 us (level)
  no operation moved by 1% of the time
where the time goes in v5:
time: 113 us; the launch traced here: 112 us
  Pallas kernels  108 us (96%)
  other arithmetic  2.6 us (2%)
    pallas_call x1, Pallas kernels, fused_step(): pl.pallas_call(functools.partial(step_kernel, Z, F, C), out_shape=(jax.Sh...  108 us
    add x1, other arithmetic, fused_step(): return (updates, DECAY_RATE * momentum + total.astype(F32))  2.6 us

profile of v5, /device:TPU:0, one launch (start us, length us, event | category | flops | bytes accessed | tf_op | source)
XLA Modules:
  0.0 112.4 jit_solution(14475121815185403594)
XLA Ops:
  0.6 0.0 copy-start
  0.6 108.2 %shard_map.50 = (bf16[8,1,24,2048]{3,2,1,0:T(8,128)(2,1)}, bf16[1,8,24,2048]{3,2,1,0:T(8,128)(2,1)}) custom-call(s32[8]{0:T(128)} %owner_ref.1, bf16[1,8,96,2048]{3,2,1,0:T(8,128)(2,1)} %grads_hbm.1, f32[1,8,24,2048]{3,2,1,0:T(8,128)} %mom_hbm.1), custom_call_target="tpu_custom_call" | custom-call | flops 2415919104 | bytes 6291456 | tf_op jit(solution)/shard_map/pallas_call | solution.py:356
  108.9 0.0 copy-done
  108.9 0.0 copy-start.1
  108.9 2.6 %convert_add_fusion = f32[1,8,24,2048]{3,2,1,0:T(8,128)} fusion(bf16[1,8,24,2048]{3,2,1,0:T(8,128)(2,1)} %get-tuple-element.5, f32[1,8,24,2048]{3,2,1,0:T(8,128)S(1)} %copy-done), kind=kLoop, calls=%fused_computation | loop fusion | flops 1179648 | bytes 3932160 | tf_op jit(solution)/shard_map/add | solution.py:397
  111.5 0.0 copy-done.1
  111.5 0.9 copy.6
Async XLA Ops:
  0.6 108.2 %copy-start = (f32[1,8,24,2048]{3,2,1,0:T(8,128)S(1)}, f32[1,8,24,2048]{3,2,1,0:T(8,128)}, u32[]{:S(2)}) copy-start(f32[1,8,24,2048]{3,2,1,0:T(8,128)} %mom_hbm.1) | copy-start | bytes 4718596
  108.9 2.6 %copy-start.1 = (bf16[8,1,24,2048]{3,2,1,0:T(8,128)(2,1)S(1)}, bf16[8,1,24,2048]{3,2,1,0:T(8,128)(2,1)}, u32[]{:S(2)}) copy-start(bf16[8,1,24,2048]{3,2,1,0:T(8,128)(2,1)} %get-tuple-element.8) | copy-start | bytes 2359300
